TPU v7x, 32 devices: a whole 2x2x4 slice. The times are simulated.
32 devices in a mesh: dm: 4 (over y, x), freq: 8 (over z, core).
Axes of the slice: x: 2, y: 2, z: 4, core: 2. Of those that a mesh axis runs over, the one named last changes fastest.
Arguments:
- series: float32 [16777216], P(('dm', 'freq')), parts along dimension 0, may hold values from -6 to 6
- kernels: float32 [2, 16, 129], replicated, may hold values from -0.5 to 0.5
- half_widths: int32 [16], replicated, may hold values from 32 to 64, as said below
- sub_rows: int32 [3, 16], replicated, may hold values from 0 to 15
Outputs:
- summed: float32 [16, 8388608], P(None, ('dm', 'freq')), parts along dimension 1
There are 4 independent parts, one for each index of `dm`. A program takes and returns all parts, laid end to end along the dimension named above; an argument that names none is the same for every part. Nothing has to cross between parts.
Inputs may be any that keep to these rules, and one draw needn't show every extreme that they name: Template t's kernel is nonzero only at offsets |j| <= half_widths[t]; some template has half-width exactly 64.
All inputs are finite; a program needn't handle non-finite values.
Results may differ from a plain program's by a relative error of at most 0.000051.
Values sent between devices are 32-bit elements; how exact they have to be, the bound alone decides.
A program may use at most 832 MiB of HBM per device.

v0:
```python
import math

import jax
import jax.numpy as jnp
from jax import lax
from jax.sharding import PartitionSpec as P

SAMPLES = 4194304
FACTOR = 2048


highest = lax.Precision.HIGHEST


def extended(block, sides, width):
    for axis, dim in sides:
        count = lax.axis_size(axis)
        forward = [(i, i + 1) for i in range(count - 1)]
        backward = [(target, source) for source, target in forward]
        low = lax.ppermute(
            lax.slice_in_dim(block, block.shape[dim] - width, None, axis=dim), axis, forward
        )
        high = lax.ppermute(lax.slice_in_dim(block, 0, width, axis=dim), axis, backward)
        block = jnp.concatenate([low, block, high], axis=dim)
    return block


def unit_table(left_ints, right_ints, length):
    product = left_ints * right_ints % length
    angles = product.astype(jnp.float32) * (-2.0 * math.pi / length)
    return (jnp.cos(angles), jnp.sin(angles))


def complex_times(left_pair, right_pair):
    return (
        left_pair[0] * right_pair[0] - left_pair[1] * right_pair[1],
        left_pair[0] * right_pair[1] + left_pair[1] * right_pair[0],
    )


def complex_einsum(pattern, left_pair, right_pair):

    def single(one_side, other_side):
        return jnp.einsum(pattern, one_side, other_side, precision=highest)

    return (
        single(left_pair[0], right_pair[0]) - single(left_pair[1], right_pair[1]),
        single(left_pair[0], right_pair[1]) + single(left_pair[1], right_pair[0]),
    )


def forward_spectrum(series, members, position):
    rows_lo = FACTOR // members
    cols_lo = series.shape[0] // rows_lo // members
    blocks = series.reshape(rows_lo, members, cols_lo)
    sendable = jnp.transpose(blocks, (1, 0, 2)).reshape(members, rows_lo * cols_lo)
    arrived = lax.all_to_all(sendable, "freq", split_axis=0, concat_axis=0, tiled=True).reshape(
        members, rows_lo, cols_lo
    )
    outer_ids = jnp.arange(members, dtype=jnp.int32)
    inner_ids = jnp.arange(rows_lo, dtype=jnp.int32)
    outer_table = unit_table(outer_ids[:, None], outer_ids[None, :], members)
    first_real = jnp.einsum("pr,rsc->psc", outer_table[0], arrived, precision=highest)
    first_imag = jnp.einsum("pr,rsc->psc", outer_table[1], arrived, precision=highest)
    turned = complex_times(
        (first_real, first_imag),
        unit_table(outer_ids[:, None, None], inner_ids[None, :, None], FACTOR),
    )
    inner_table = unit_table(inner_ids[:, None], inner_ids[None, :], rows_lo)
    columns = complex_einsum("qs,psc->cqp", inner_table, turned)
    column_ids = jnp.arange(cols_lo, dtype=jnp.int32) + position * cols_lo
    frequency_ids = jnp.arange(FACTOR, dtype=jnp.int32)
    columns = complex_times(
        (columns[0].reshape(cols_lo, FACTOR), columns[1].reshape(cols_lo, FACTOR)),
        unit_table(column_ids[:, None], frequency_ids[None, :], SAMPLES),
    )

    def arrange(values):
        return jnp.transpose(values.reshape(cols_lo, members, rows_lo), (1, 2, 0)).reshape(
            members, rows_lo * cols_lo
        )

    arrived = (
        lax.all_to_all(arrange(columns[0]), "freq", split_axis=0, concat_axis=0, tiled=True),
        lax.all_to_all(arrange(columns[1]), "freq", split_axis=0, concat_axis=0, tiled=True),
    )
    cube = (
        arrived[0].reshape(members, rows_lo, cols_lo),
        arrived[1].reshape(members, rows_lo, cols_lo),
    )
    second = complex_einsum("pr,ras->pas", outer_table, cube)
    lane_ids = jnp.arange(cols_lo, dtype=jnp.int32)
    turned = complex_times(
        second, unit_table(outer_ids[:, None, None], lane_ids[None, None, :], members * cols_lo)
    )
    row_block = cols_lo // 2
    last_table = unit_table(
        jnp.arange(row_block, dtype=jnp.int32)[:, None], lane_ids[None, :], cols_lo
    )
    spectrum = complex_einsum("qs,pas->qpa", last_table, turned)
    norming = 1.0 / math.sqrt(SAMPLES)
    rows_pair = (
        (spectrum[0] * norming).reshape(row_block * members, rows_lo),
        (spectrum[1] * norming).reshape(row_block * members, rows_lo),
    )
    return (rows_pair, row_block, rows_lo)


def toeplitz(kernels, half_widths):
    tap_count = kernels.shape[2]
    half_span = tap_count // 2
    stride = 2 * half_span
    offsets = jnp.abs(jnp.arange(tap_count, dtype=jnp.int32) - half_span)
    inside = offsets[None, :] <= half_widths[:, None]
    masked = jnp.where(inside[None, :, :], kernels, jnp.zeros_like(kernels))
    length = stride + tap_count
    padded = jnp.pad(masked, ((0, 0), (0, 0), (0, stride)))
    repeated = jnp.tile(padded, (1, 1, stride))[:, :, : stride * (length - 1)]
    return repeated.reshape(2, kernels.shape[1], stride, length - 1)


def correlate(rimmed, matrices):
    stride = matrices.shape[2]
    templates = matrices.shape[1]
    length = rimmed.shape[1] - stride
    block_count = length // stride
    head_rows = rimmed[:, :length].reshape(2, block_count, stride)
    tail_rows = rimmed[:, stride : stride + length].reshape(2, block_count, stride)
    windows = jnp.concatenate([head_rows[0], tail_rows[0], head_rows[1], tail_rows[1]], axis=1)
    real_part = jnp.transpose(matrices[0], (2, 0, 1))
    imag_part = jnp.transpose(matrices[1], (2, 0, 1))
    upper = jnp.stack([real_part, imag_part], axis=1)
    lower = jnp.stack([-imag_part, real_part], axis=1)
    stacked = jnp.concatenate([upper, lower], axis=0).reshape(4 * stride, 2 * templates * stride)
    response = jnp.dot(windows, stacked, precision=highest, preferred_element_type=jnp.float32)
    response = response.reshape(block_count, 2, templates, stride)
    powers = response[:, 0] * response[:, 0] + response[:, 1] * response[:, 1]
    return jnp.transpose(powers, (1, 0, 2)).reshape(templates, length)


def combine(plane_rows, pulled, quarter):
    templates = plane_rows.shape[0]
    fourths = plane_rows.reshape(templates, quarter, 4)
    single_rate = pulled[0].reshape(templates, quarter, 1)
    double_rate = pulled[1].reshape(templates, quarter, 2)
    triple_rate = pulled[2].reshape(templates, quarter, 3)
    doubled = jnp.concatenate(
        [
            double_rate[:, :, 0:1],
            double_rate[:, :, 0:1],
            double_rate[:, :, 1:2],
            double_rate[:, :, 1:2],
        ],
        axis=2,
    )
    tripled = jnp.concatenate(
        [
            triple_rate[:, :, 0:1],
            triple_rate[:, :, 0:1],
            triple_rate[:, :, 1:2],
            triple_rate[:, :, 2:3],
        ],
        axis=2,
    )
    return (fourths + single_rate + doubled + tripled).reshape(templates, 4 * quarter)


def on_device(series, kernels, half_widths, sub_rows):
    members = lax.axis_size("freq")
    position = lax.axis_index("freq")
    rows_pair, row_block, freq_rows = forward_spectrum(series, members, position)
    half_span = kernels.shape[2] // 2
    bins_local = row_block * FACTOR
    arrived = (
        lax.all_to_all(
            rows_pair[0].reshape(members, row_block * freq_rows),
            "freq",
            split_axis=0,
            concat_axis=0,
            tiled=True,
        ),
        lax.all_to_all(
            rows_pair[1].reshape(members, row_block * freq_rows),
            "freq",
            split_axis=0,
            concat_axis=0,
            tiled=True,
        ),
    )

    def assemble(values):
        return jnp.transpose(values.reshape(members, row_block, freq_rows), (1, 0, 2)).reshape(
            bins_local
        )

    rimmed = extended(
        jnp.stack([assemble(arrived[0]), assemble(arrived[1])]), (("freq", 1),), half_span
    )
    matrices = toeplitz(kernels, half_widths)
    plane_rows = correlate(rimmed, matrices)
    quarter = bins_local // 4
    sub_run = quarter // members
    own_bins = rimmed[:, half_span : half_span + bins_local]
    holdings = lax.all_to_all(
        own_bins.reshape(2, 4, members, sub_run), "freq", split_axis=2, concat_axis=1, tiled=True
    )
    holdings = jnp.pad(holdings.reshape(2, 4 * members, sub_run), ((0, 0), (1, 0), (0, 0)))
    pieces = []
    for harmonic in range(1, 4):
        pieces.extend(
            (
                holdings[:, offset : offset + harmonic * members : harmonic]
                for offset in range(harmonic + 2)
            )
        )
    arrived = lax.all_to_all(
        jnp.stack(pieces, axis=1), "freq", split_axis=2, concat_axis=2, tiled=True
    )
    pulled = []
    first_slot = 0
    for harmonic in range(1, 4):
        stretch = arrived[:, first_slot : first_slot + harmonic + 2].reshape(
            2, (harmonic + 2) * quarter
        )
        first_slot = first_slot + harmonic + 2
        window_part = stretch[:, quarter - half_span : quarter + harmonic * quarter + half_span]
        pulled.append(correlate(window_part, jnp.take(matrices, sub_rows[harmonic - 1], axis=1)))
    return combine(plane_rows, pulled, quarter)


def solution(mesh):
    in_specs = (P(("dm", "freq")), P(), P(), P())
    out_specs = P(None, ("dm", "freq"))
    return jax.shard_map(
        on_device, mesh=mesh, in_specs=in_specs, out_specs=out_specs, check_vma=False
    )
```

profile of v0, /device:TPU:1, one launch (start us, length us, event | category | flops | bytes accessed | tf_op | source)
XLA Modules:
  0.0 1573.2 jit_solution(9394914630861904804)
XLA Ops:
  1.9 3.5 copy.282
  5.4 6.5 all-to-all-start
  12.3 47.8 %all-to-all-done = f32[8,1,65536]{2,1,0:T(1,128)} async-done(((f32[8,1,65536]{2,1,0:T(1,128)}), f32[8,1,65536]{2,1,0:T(1,128)}, u32[]{:S(2)}, u32[]{:S(2)}) %all-to-all-start) | async-done | bytes 2097184 | tf_op jit(solution)/shard_map/all_to_all | solution.py:57
  60.1 6.6 reduce
  71.1 3.8 fusion.75
  75.0 3.4 fusion.77
  78.4 3.5 subtract_bitcast_fusion
  81.9 3.6 add_bitcast_fusion
  88.1 10.0 fusion.64
  98.1 6.6 all_to_all.58
  104.7 5.1 all-to-all-start.1
  109.8 4.2 all_to_all.59
  114.0 44.2 %all-to-all-done.1 = f32[8,1,65536]{2,1,0:T(1,128)} async-done(((f32[8,1,65536]{2,1,0:T(1,128)}), f32[8,1,65536]{2,1,0:T(1,128)}, u32[]{:S(2)}, u32[]{:S(2)}) %all-to-all-start.1) | async-done | bytes 2097184 | tf_op jit(solution)/shard_map/all_to_all | solution.py:84
  158.1 5.1 all-to-all-start.2
  163.2 6.6 reduce.1
  169.8 3.2 fusion.156
  173.0 38.6 %all-to-all-done.2 = f32[8,1,65536]{2,1,0:T(1,128)} async-done(((f32[8,1,65536]{2,1,0:T(1,128)}), f32[8,1,65536]{2,1,0:T(1,128)}, u32[]{:S(2)}, u32[]{:S(2)}) %all-to-all-start.2) | async-done | bytes 2097184 | tf_op jit(solution)/shard_map/all_to_all | solution.py:85
  211.6 7.0 reduce.2
  224.9 3.1 fusion.69
  228.0 3.1 fusion.96
  233.9 4.3 all-to-all-start.3
  238.4 3.1 tile.4
  241.5 6.7 tile.10
  248.1 4.6 fusion.67
  252.8 3.1 fusion.93
  258.5 5.4 all-to-all-done.3
  264.0 4.6 all-to-all-start.4
  268.6 4.5 fusion.234
  276.6 17.7 %all-to-all-done.4 = f32[8,1,32768]{2,1,0:T(1,128)S(1)} async-done(((f32[8,1,32768]{2,1,0:T(1,128)}), f32[8,1,32768]{2,1,0:T(1,128)S(1)}, u32[]{:S(2)}, u32[]{:S(2)}) %all-to-all-start.4) | async-done | bytes 1048608 | tf_op jit(solution)/shard_map/all_to_all | solution.py:182
  300.5 2.7 copy.311
  303.2 5.6 all-to-all-start.5
  315.3 3.3 copy.339
  318.6 5.0 gather_fusion.2
  323.7 5.0 gather_fusion.1
  328.7 5.0 gather_fusion
  333.7 3.3 fusion.62
  337.0 3.4 select_bitcast_fusion
  356.2 3.5 collective-permute-start
  361.7 3.2 copy.312
  374.9 6.2 copy.313
  381.1 5.2 all-to-all-start.6
  386.3 22.2 %pad_maximum_fusion.8 = (f32[1,262144]{1,0:T(1,128)S(1)}, f32[1,262144]{1,0:T(1,128)S(1)}, f32[1,262144]{1,0:T(1,128)S(1)}, f32[1,262144]{1,0:T(1,128)S(1)}) fusion(f32[2,64]{1,0:T(2,128)S(1)} %collective-permute-done, f32[1,262144]{1,0:T(1,128)S(1)} %stack_reshape.7, f32[1,262144]{1,0:T(1,128)S(1)} %stack_reshape.6, f32[2,64]{1,0:T(2,128)S(1)} %collective-permute-done.1), kind=kLoop, calls=%fused_computation.149 | loop fusion | flops 2097152 | bytes 6292480 | tf_op jit(solution)/shard_map/slice | solution.py:129
  408.6 58.2 %fusion.8 = f32[2048,2,16,128]{3,0,2,1:T(8,128)} fusion(f32[256,1,16,128]{0,3,2,1:T(8,128)S(1)} %bitcast.387, f32[256,1,16,128]{0,3,2,1:T(8,128)S(1)} %copy-done.13, f32[256,1,16,128]{0,3,2,1:T(8,128)S(1)} %bitcast.375, f32[2048,128]{1,0:T(8,128)S(1)} %bitcast.390, f32[2048,128]{1,0:T(8,128)S(1)} %bitcast.389, f32[2048,128]{1,0:T(8,128)S(1)} %bitcast.391, ...), kind=kOutput, calls=%fused_computation.21 | convolution fusion | flops 51549044736 | bytes 44040192 | tf_op jit(solution)/shard_map/dot_general | solution.py:135
  466.8 17.8 %fusion.3 = f32[16,2048,128]{2,1,0:T(8,128)} fusion(f32[2048,2,16,128]{3,0,2,1:T(8,128)} %fusion.8), kind=kLoop, calls=%fused_computation.10 | loop fusion | flops 12582912 | bytes 50331648 | tf_op jit(solution)/shard_map/transpose | solution.py:138
  484.6 61.5 %copy.329 = f32[16,2048,128]{0,2,1:T(8,128)} copy(f32[16,2048,128]{2,1,0:T(8,128)} %fusion.3) | data formatting | bytes 33554432 | tf_op jit(solution)/shard_map/reshape;reshape | solution.py:143
  552.0 14.4 fusion.15
  566.4 2.6 fusion.37
  579.4 4.4 fusion.236
  583.8 7.5 fusion.235
  591.3 29.4 %fusion.22 = f32[1024,2,16,128]{3,0,2,1:T(8,128)S(1)} fusion(f32[256,1,16,128]{0,3,2,1:T(8,128)S(1)} %copy-done.15, f32[256,1,16,128]{0,3,2,1:T(8,128)S(1)} %copy-done.10, f32[256,1,16,128]{0,3,2,1:T(8,128)S(1)} %copy-done.14, f32[1024,128]{1,0:T(8,128)S(1)} %bitcast.397, f32[1024,128]{1,0:T(8,128)S(1)} %bitcast.398, f32[1024,128]{1,0:T(8,128)S(1)} %bitcast.399, ...), kind=kOutput, calls=%fused_computation.37 | convolution fusion | flops 25777668096 | bytes 25165824 | tf_op jit(solution)/shard_map/dot_general | solution.py:135
  620.7 3.8 fusion.7
  624.5 45.3 %fusion.29 = f32[1536,2,16,128]{3,0,2,1:T(8,128)S(1)} fusion(f32[256,1,16,128]{0,3,2,1:T(8,128)} %get-tuple-element.27, f32[256,1,16,128]{0,3,2,1:T(8,128)S(1)} %copy-done.9, f32[256,1,16,128]{0,3,2,1:T(8,128)} %get-tuple-element.26, f32[1536,128]{1,0:T(8,128)S(1)} %bitcast.393, f32[1536,128]{1,0:T(8,128)} %bitcast.394, f32[1536,128]{1,0:T(8,128)} %bitcast.395, ...), kind=kOutput, calls=%fused_computation.45 | convolution fusion | flops 38663356416 | bytes 34603008 | tf_op jit(solution)/shard_map/dot_general | solution.py:135
  669.8 5.2 fusion.5
  675.0 17.1 %copy.330 = f32[16,512,128]{0,2,1:T(8,128)} copy(f32[16,512,128]{2,1,0:T(8,128)} %fusion.37) | data formatting | bytes 8388608 | tf_op jit(solution)/shard_map/add | solution.py:165
  692.1 31.7 %copy.320 = f32[16,1024,128]{0,2,1:T(8,128)} copy(f32[16,1024,128]{2,1,0:T(8,128)} %fusion.7) | data formatting | bytes 16777216 | tf_op jit(solution)/shard_map/transpose | solution.py:138
  723.8 64.2 %fusion.233 = (f32[16,65536,1]{0,2,1:T(1,128)}, f32[16,65536,1]{0,2,1:T(1,128)}) fusion(f32[16,65536,2]{0,2,1:T(2,128)} %bitcast.97), kind=kLoop, calls=%fused_computation.311 | loop fusion | bytes 16777216 | tf_op jit(solution)/shard_map/slice | solution.py:149
  788.0 46.8 %copy.323 = f32[16,1536,128]{0,2,1:T(8,128)} copy(f32[16,1536,128]{2,1,0:T(8,128)} %fusion.5) | data formatting | bytes 25165824 | tf_op jit(solution)/shard_map/transpose | solution.py:138
  834.8 146.2 %reshape_reshape.14 = f32[16,65536,3]{0,2,1:T(4,128)} reshape(f32[16,1536,128]{0,2,1:T(8,128)} %copy.323) | data formatting | bytes 25165824 | tf_op jit(solution)/shard_map/reshape;reshape | solution.py:146
  981.1 52.1 %slice.338 = f32[16,65536,1]{0,2,1:T(1,128)} slice(f32[16,65536,3]{0,2,1:T(4,128)} %reshape_reshape.14), slice={[0:16], [0:65536], [0:1]} | slice | bytes 8388608 | tf_op jit(solution)/shard_map/slice | solution.py:158
  1033.2 96.9 %pad_maximum_fusion.1 = f32[16,65536,4]{0,2,1:T(4,128)} fusion(f32[16,65536,3]{0,2,1:T(4,128)} %reshape_reshape.14, f32[16,65536,1]{0,2,1:T(1,128)} %slice.338), kind=kLoop, calls=%fused_computation.4 | loop fusion | flops 4194304 | bytes 33554432 | tf_op jit(solution)/shard_map/concatenate | solution.py:156
  1130.1 116.0 %pad_maximum_fusion = f32[16,65536,4]{0,2,1:T(4,128)} fusion(f32[16,65536,1]{0,2,1:T(1,128)} %get-tuple-element.13, f32[16,65536,2]{0,2,1:T(2,128)} %bitcast.97, f32[16,65536,1]{0,2,1:T(1,128)} %get-tuple-element.12), kind=kLoop, calls=%fused_computation.3 | loop fusion | flops 8388608 | bytes 33554432 | tf_op jit(solution)/shard_map/concatenate | solution.py:147
  1246.1 53.1 %add.201 = f32[16,65536,4]{0,2,1:T(4,128)} broadcast(f32[16,65536]{0,1:T(8,128)} %bitcast.360), dimensions={0,1} | broadcast | bytes 20971520 | tf_op jit(solution)/shard_map/add | solution.py:165
  1299.2 203.5 %fusion.1 = f32[16,262144]{0,1:T(8,128)} fusion(f32[16,262144]{0,1:T(8,128)} %bitcast.122, f32[16,262144]{0,1:T(8,128)} %bitcast.98, f32[16,262144]{0,1:T(8,128)} %bitcast.73, f32[16,2048,128]{0,2,1:T(8,128)} %copy.329), kind=kLoop, calls=%fused_computation.7 | loop fusion | flops 12582912 | bytes 83886080 | tf_op jit(solution)/shard_map/add | solution.py:165
  1502.8 70.2 %copy.324 = f32[16,262144]{1,0:T(8,128)} copy(f32[16,262144]{0,1:T(8,128)} %fusion.1) | data formatting | bytes 33554432 | tf_op jit(solution)/shard_map/add | solution.py:165
  (117 shorter events, 81.3 us)
Async XLA Ops:
  5.4 54.7 %all-to-all-start = ((f32[8,1,65536]{2,1,0:T(1,128)}), f32[8,1,65536]{2,1,0:T(1,128)}, u32[]{:S(2)}, u32[]{:S(2)}) async-start(f32[8,1,65536]{2,1,0:T(1,128)} %copy.282), calls=%async_computation | async-start | bytes 4194304 | tf_op jit(solution)/shard_map/all_to_all | solution.py:57
  104.7 53.4 %all-to-all-start.1 = ((f32[8,1,65536]{2,1,0:T(1,128)}), f32[8,1,65536]{2,1,0:T(1,128)}, u32[]{:S(2)}, u32[]{:S(2)}) async-start(f32[8,1,65536]{2,1,0:T(1,128)} %all_to_all.58), calls=%async_computation.1 | async-start | bytes 4194304 | tf_op jit(solution)/shard_map/all_to_all | solution.py:84
  158.1 53.4 %all-to-all-start.2 = ((f32[8,1,65536]{2,1,0:T(1,128)}), f32[8,1,65536]{2,1,0:T(1,128)}, u32[]{:S(2)}, u32[]{:S(2)}) async-start(f32[8,1,65536]{2,1,0:T(1,128)} %all_to_all.59), calls=%async_computation.2 | async-start | bytes 4194304 | tf_op jit(solution)/shard_map/all_to_all | solution.py:85
  169.8 3.2 copy-start.1
  218.5 1.9 copy-start.5
  220.4 2.0 copy-start.2
  224.9 6.2 copy-start
  231.9 6.4 copy-start.20
  231.9 6.5 copy-start.18
  233.9 30.1 %all-to-all-start.3 = ((f32[8,1,32768]{2,1,0:T(1,128)}), f32[8,1,32768]{2,1,0:T(1,128)S(1)}, u32[]{:S(2)}, u32[]{:S(2)}) async-start(f32[8,1,32768]{2,1,0:T(1,128)} %all_to_all.60), calls=%async_computation.3 | async-start | bytes 2097152 | tf_op jit(solution)/shard_map/all_to_all | solution.py:175
  264.0 30.3 %all-to-all-start.4 = ((f32[8,1,32768]{2,1,0:T(1,128)}), f32[8,1,32768]{2,1,0:T(1,128)S(1)}, u32[]{:S(2)}, u32[]{:S(2)}) async-start(f32[8,1,32768]{2,1,0:T(1,128)} %all_to_all.61), calls=%async_computation.4 | async-start | bytes 2097152 | tf_op jit(solution)/shard_map/all_to_all | solution.py:182
  268.6 4.5 copy-start.19
  303.2 58.4 %all-to-all-start.5 = ((f32[2,4,8,8192]{3,1,0,2:T(4,128)}), f32[2,4,8,8192]{3,1,0,2:T(4,128)}, u32[]{:S(2)}, u32[]{:S(2)}) async-start(f32[2,4,8,8192]{3,1,0,2:T(4,128)} %copy.311), calls=%async_computation.5 | async-start | bytes 4194304 | tf_op jit(solution)/shard_map/all_to_all | solution.py:204
  308.8 1.6 copy-start.8
  310.4 1.9 copy-start.7
  312.4 2.9 slice-start
  333.7 3.3 copy-start.4
  341.8 2.9 copy-start.3
  356.2 30.1 %collective-permute-start = (f32[2,64]{1,0:T(2,128)S(1)}, f32[2,64]{1,0:T(2,128)S(1)}, u32[]{:S(2)}, u32[]{:S(2)}) collective-permute-start(f32[2,64]{1,0:T(2,128)S(1)} %get-tuple-element.38), channel_id=1, source_target_pairs={{0,1},{1,2},{2,3},{3,4},{4,5},{5,6},{6,7},{8,9},{9,10},{10,11},{11... | collective-permute-start | bytes 1544 | tf_op jit(solution)/shard_map/ppermute | solution.py:20
  359.7 26.6 %collective-permute-start.1 = (f32[2,64]{1,0:T(2,128)S(1)}, f32[2,64]{1,0:T(2,128)S(1)}, u32[]{:S(2)}, u32[]{:S(2)}) collective-permute-start(f32[2,64]{1,0:T(2,128)S(1)} %get-tuple-element.39), channel_id=1, source_target_pairs={{1,0},{2,1},{3,2},{4,3},{5,4},{6,5},{7,6},{9,8},{10,9},{11,10},{12... | collective-permute-start | bytes 1544 | tf_op jit(solution)/shard_map/ppermute | solution.py:23
  381.1 165.0 %all-to-all-start.6 = ((f32[2,12,8,8192]{3,0,1,2:T(2,128)}), f32[2,12,8,8192]{3,0,1,2:T(2,128)}, u32[]{:S(2)}, u32[]{:S(2)}) async-start(f32[2,12,8,8192]{3,0,1,2:T(2,128)} %copy.313), calls=%async_computation.6 | async-start | bytes 12582912 | tf_op jit(solution)/shard_map/all_to_all | solution.py:216
  386.3 22.2 %copy-start.6 = (f32[2,8,128,256]{3,2,1,0:T(8,128)S(1)}, f32[2,8,128,256]{3,2,1,0:T(8,128)}, u32[]{:S(2)}) copy-start(f32[2,8,128,256]{3,2,1,0:T(8,128)} %copy.337) | copy-start | bytes 6291460
  386.3 22.2 %copy-start.12 = (f32[2,8,128,256]{3,2,1,0:T(8,128)S(1)}, f32[2,8,128,256]{3,2,1,0:T(8,128)}, u32[]{:S(2)}) copy-start(f32[2,8,128,256]{3,2,1,0:T(8,128)} %copy.336) | copy-start | bytes 6291460
  386.3 22.2 %copy-start.13 = (f32[256,1,16,128]{0,3,2,1:T(8,128)S(1)}, f32[256,1,16,128]{0,3,2,1:T(8,128)}, u32[]{:S(2)}) copy-start(f32[256,1,16,128]{0,3,2,1:T(8,128)} %fusion.62) | copy-start | bytes 6291460
  547.6 4.4 copy-start.17
  548.5 3.5 copy-start.11
  548.5 3.5 copy-start.16
  583.8 7.5 copy-start.10
  583.8 7.5 copy-start.14
  583.8 7.5 copy-start.15
  620.7 3.8 copy-start.9
where the time goes:
time: 1590 us; the launch traced here: 1570 us
  local copies, waits for them, and re-layouts  671 us (42%)
  other arithmetic  517 us (33%)
  matrix products  189 us (12%)
  waiting for transfers between devices  154 us (10%)
  starting transfers between devices  41.9 us (3%)
    add x1, other arithmetic, combine(): fourths + single_rate + doubled + tripled  204 us
    dot_general x4, matrix products, correlate(): jnp.dot(windows, stacked, precision=highest, preferred_element_type=jnp.f...  147 us
    another operation x1, local copies, waits for them, and re-layouts, combine(): triple_rate = pulled[2].reshape(templates, quarter, 3)  146 us
    add x3, local copies, waits for them, and re-layouts, combine(): fourths + single_rate + doubled + tripled  140 us
    concatenate x1, other arithmetic, combine(): jnp.concatenate([double_rate[:, :, 0:1], double_rate[:, :, 0:1], double_r...  116 us
    concatenate x1, other arithmetic, combine(): jnp.concatenate([triple_rate[:, :, 0:1], triple_rate[:, :, 0:1], triple_r...  96.9 us
    transpose x2, local copies, waits for them, and re-layouts, correlate(): return jnp.transpose(powers, (1, 0, 2)).reshape(templates, length)  78.6 us
    slice x1, local copies, waits for them, and re-layouts, combine(): double_rate[:, :, 0:1]  64.2 us
  transfers between devices with their start and end apart: 9, of which 5 were waited for; matrix products, arithmetic and copies ran while one was open for 16% of the time, Pallas kernels for 0%

commit v1 on v0

v1 whole, which is shorter than its diff:
```python
import functools
import math

import jax
import jax.numpy as jnp
import numpy as np
from jax import lax
from jax.experimental import pallas as pl
from jax.experimental.pallas import tpu as pltpu
from jax.sharding import PartitionSpec as P

FACTOR = 2048
LANES = 128
GROUP = 8


highest = lax.Precision.HIGH


def unit_table(left_ints, right_ints, length):
    product = left_ints * right_ints % length
    angles = product.astype(jnp.float32) * (-2.0 * math.pi / length)
    return (jnp.cos(angles), jnp.sin(angles))


def complex_times(left_pair, right_pair):
    return (
        left_pair[0] * right_pair[0] - left_pair[1] * right_pair[1],
        left_pair[0] * right_pair[1] + left_pair[1] * right_pair[0],
    )


def complex_einsum(pattern, left_pair, right_pair):

    def single(one_side, other_side):
        return jnp.einsum(pattern, one_side, other_side, precision=highest)

    return (
        single(left_pair[0], right_pair[0]) - single(left_pair[1], right_pair[1]),
        single(left_pair[0], right_pair[1]) + single(left_pair[1], right_pair[0]),
    )


def forward_spectrum(series, members, position):
    samples = members * series.shape[0]
    rows_lo = FACTOR // members
    cols_lo = series.shape[0] // rows_lo // members
    blocks = series.reshape(rows_lo, members, cols_lo)
    sendable = jnp.transpose(blocks, (1, 0, 2)).reshape(members, rows_lo * cols_lo)
    arrived = lax.all_to_all(sendable, "freq", split_axis=0, concat_axis=0, tiled=True).reshape(
        members, rows_lo, cols_lo
    )
    outer_ids = jnp.arange(members, dtype=jnp.int32)
    inner_ids = jnp.arange(rows_lo, dtype=jnp.int32)
    outer_table = unit_table(outer_ids[:, None], outer_ids[None, :], members)
    first_real = jnp.einsum("pr,rsc->psc", outer_table[0], arrived, precision=highest)
    first_imag = jnp.einsum("pr,rsc->psc", outer_table[1], arrived, precision=highest)
    turned = complex_times(
        (first_real, first_imag),
        unit_table(outer_ids[:, None, None], inner_ids[None, :, None], FACTOR),
    )
    inner_table = unit_table(inner_ids[:, None], inner_ids[None, :], rows_lo)
    columns = complex_einsum("qs,psc->cqp", inner_table, turned)
    column_ids = jnp.arange(cols_lo, dtype=jnp.int32) + position * cols_lo
    frequency_ids = jnp.arange(FACTOR, dtype=jnp.int32)
    columns = complex_times(
        (columns[0].reshape(cols_lo, FACTOR), columns[1].reshape(cols_lo, FACTOR)),
        unit_table(column_ids[:, None], frequency_ids[None, :], samples),
    )

    def arrange(values):
        return jnp.transpose(values.reshape(cols_lo, members, rows_lo), (1, 2, 0)).reshape(
            members, rows_lo * cols_lo
        )

    arrived = (
        lax.all_to_all(arrange(columns[0]), "freq", split_axis=0, concat_axis=0, tiled=True),
        lax.all_to_all(arrange(columns[1]), "freq", split_axis=0, concat_axis=0, tiled=True),
    )
    cube = (
        arrived[0].reshape(members, rows_lo, cols_lo),
        arrived[1].reshape(members, rows_lo, cols_lo),
    )
    second = complex_einsum("pr,ras->pas", outer_table, cube)
    lane_ids = jnp.arange(cols_lo, dtype=jnp.int32)
    turned = complex_times(
        second, unit_table(outer_ids[:, None, None], lane_ids[None, None, :], members * cols_lo)
    )
    row_block = cols_lo // 2
    last_table = unit_table(
        jnp.arange(row_block, dtype=jnp.int32)[:, None], lane_ids[None, :], cols_lo
    )
    spectrum = complex_einsum("qs,pas->qpa", last_table, turned)
    norming = 1.0 / math.sqrt(samples)
    rows_pair = (
        (spectrum[0] * norming).reshape(row_block * members, rows_lo),
        (spectrum[1] * norming).reshape(row_block * members, rows_lo),
    )
    return (rows_pair, row_block, rows_lo)


def toeplitz(kernels, half_widths):
    tap_count = kernels.shape[2]
    half_span = tap_count // 2
    stride = 2 * half_span
    offsets = jnp.abs(jnp.arange(tap_count, dtype=jnp.int32) - half_span)
    inside = offsets[None, :] <= half_widths[:, None]
    masked = jnp.where(inside[None, :, :], kernels, jnp.zeros_like(kernels))
    length = stride + tap_count
    padded = jnp.pad(masked, ((0, 0), (0, 0), (0, stride)))
    repeated = jnp.tile(padded, (1, 1, stride))[:, :, : stride * (length - 1)]
    return repeated.reshape(2, kernels.shape[1], stride, length - 1)


def split_halves(values):
    rounded = lax.reduce_precision(values, exponent_bits=8, mantissa_bits=7)
    return rounded.astype(jnp.bfloat16), (values - rounded).astype(jnp.bfloat16)


def reach(harmonic, half_span):
    return harmonic * LANES // 4 + 2 * half_span


def padded_depth(harmonic, half_span):
    return -(-2 * reach(harmonic, half_span) // LANES) * LANES


def weights(matrices, harmonic, half_span):
    width = reach(harmonic, half_span)
    picks = np.arange(LANES) * harmonic // 4
    chosen = jnp.asarray(np.arange(LANES)[:, None] == picks[None, :], jnp.bfloat16)
    result = []
    for half in split_halves(matrices):
        turned = jnp.einsum(
            "ctmi,ml->ctil", half[..., :width], chosen, preferred_element_type=jnp.float32
        ).astype(jnp.bfloat16)
        real, imag = turned[0], turned[1]
        upper = jnp.concatenate([real, imag], axis=2)
        lower = jnp.concatenate([-imag, real], axis=2)
        both = jnp.concatenate([upper, lower], axis=1)
        extra = padded_depth(harmonic, half_span) - 2 * width
        result.append(jnp.pad(both, ((0, 0), (0, extra), (0, 0))))
    return result


def windows(stretch, harmonic, half_span, blocks):
    step = harmonic * LANES // 4
    width = reach(harmonic, half_span)
    count = -(-width // step)
    short = max(0, (blocks + count - 1) * step - stretch.shape[1])
    stretch = jnp.pad(stretch, ((0, 0), (0, short)))
    pieces = []
    for part in range(2):
        for piece in range(count):
            taken = stretch[part, piece * step : (piece + blocks) * step].reshape(blocks, step)
            pieces.append(taken[:, : min(step, width - piece * step)])
    extra = padded_depth(harmonic, half_span) - 2 * width
    if extra:
        pieces.append(jnp.zeros((blocks, extra), stretch.dtype))
    return jnp.concatenate(pieces, axis=1)


def power_kernel(count, has_base, *refs):
    window_refs = refs[:count]
    weight_refs = refs[count : 3 * count]
    base_ref = refs[3 * count] if has_base else None
    out_ref = refs[3 * count + has_base]
    high_refs = refs[3 * count + has_base + 1 : -1][:count]
    low_refs = refs[3 * count + has_base + 1 : -1][count:]
    held = refs[-1]
    rows = window_refs[0].shape[0]
    for index in range(count):
        values = window_refs[index][...]
        rounded = values.astype(jnp.bfloat16)
        high_refs[index][...] = rounded
        low_refs[index][...] = (values - rounded.astype(jnp.float32)).astype(jnp.bfloat16)
    for template in range(GROUP):
        total = None
        for index in range(count):
            high = weight_refs[2 * index][template]
            low = weight_refs[2 * index + 1][template]
            left = high_refs[index][...]

            def product(one, other):
                return jnp.dot(one, other, preferred_element_type=jnp.float32)

            response = product(left, high) + (
                product(low_refs[index][...], high) + product(left, low)
            )
            real, imag = response[:, :LANES], response[:, LANES:]
            power = real * real + imag * imag
            total = power if total is None else total + power
        held[pl.ds(template, rows, stride=GROUP), :] = total
    for row in range(rows):
        values = held[row * GROUP : (row + 1) * GROUP, :]
        place = slice(row * LANES, (row + 1) * LANES)
        if has_base:
            values = values + base_ref[:, place]
        out_ref[:, place] = values


def powers(window_list, weight_list, base):
    count = len(window_list)
    blocks = window_list[0].shape[0]
    templates = weight_list[0].shape[0]
    rows = min(256, blocks)
    depths = [window.shape[1] for window in window_list]
    in_specs = [pl.BlockSpec((rows, depth), lambda t, m: (m, 0)) for depth in depths]
    in_specs += [
        pl.BlockSpec((GROUP, weight.shape[1], 2 * LANES), lambda t, m: (t, 0, 0))
        for weight in weight_list
    ]
    out_spec = pl.BlockSpec((GROUP, rows * LANES), lambda t, m: (t, m))
    operands = [*window_list, *weight_list]
    aliases = {}
    if base is not None:
        in_specs.append(out_spec)
        aliases = {len(operands): 0}
        operands.append(base)
    flops = 2 * 3 * blocks * sum(depths) * templates * 2 * LANES
    return pl.pallas_call(
        functools.partial(power_kernel, count, int(base is not None)),
        out_shape=jax.ShapeDtypeStruct((templates, blocks * LANES), jnp.float32),
        grid=(templates // GROUP, blocks // rows),
        in_specs=in_specs,
        out_specs=out_spec,
        scratch_shapes=[pltpu.VMEM((rows, depth), jnp.bfloat16) for depth in depths] * 2
        + [pltpu.VMEM((rows * GROUP, LANES), jnp.float32)],
        input_output_aliases=aliases,
        compiler_params=pltpu.CompilerParams(vmem_limit_bytes=58 * 1024 * 1024),
        cost_estimate=pl.CostEstimate(
            flops=flops,
            bytes_accessed=4 * blocks * (2 * sum(depths) + templates * LANES),
            transcendentals=0,
        ),
    )(*operands)


def fetched(rows_pair, members, ranges):
    freq_rows = rows_pair[0].shape[1]
    both = jnp.stack([jnp.pad(rows, ((1, 1), (0, 0))) for rows in rows_pair])
    total = sum(count + 2 for _, count in ranges)
    extra = -total % 8
    slabs = []
    for target in range(members):
        pieces = [both[:, target * count : target * count + count + 2] for _, count in ranges]
        pieces.append(jnp.zeros((2, extra, freq_rows), both.dtype))
        slabs.append(jnp.concatenate(pieces, axis=1))
    arrived = lax.all_to_all(jnp.stack(slabs), "freq", split_axis=0, concat_axis=0, tiled=True)
    lined = jnp.transpose(arrived, (1, 2, 0, 3)).reshape(2, total + extra, members * freq_rows)
    result = []
    first = 0
    for _, count in ranges:
        result.append(
            lined[:, first : first + count + 2].reshape(2, (count + 2) * members * freq_rows)
        )
        first += count + 2
    return result


def on_device(series, kernels, half_widths, sub_rows):
    members = lax.axis_size("freq")
    position = lax.axis_index("freq")
    rows_pair, row_block, freq_rows = forward_spectrum(series, members, position)
    half_span = kernels.shape[2] // 2
    blocks = row_block * FACTOR // LANES
    matrices = toeplitz(kernels, half_widths)

    def cut(stretch):
        return stretch[:, FACTOR - half_span :]

    own = fetched(rows_pair, members, [(4, row_block)])
    lower = fetched(rows_pair, members, [(h, h * row_block // 4) for h in range(1, 4)])
    plane = powers(
        [windows(cut(own[0]), 4, half_span, blocks)], weights(matrices, 4, half_span), None
    )
    window_list, weight_list = [], []
    for harmonic in range(1, 4):
        window_list.append(windows(cut(lower[harmonic - 1]), harmonic, half_span, blocks))
        chosen = jnp.take(matrices, sub_rows[harmonic - 1], axis=1)
        weight_list.extend(weights(chosen, harmonic, half_span))
    return powers(window_list, weight_list, plane)


def solution(mesh):
    in_specs = (P(("dm", "freq")), P(), P(), P())
    out_specs = P(None, ("dm", "freq"))
    return jax.shard_map(
        on_device, mesh=mesh, in_specs=in_specs, out_specs=out_specs, check_vma=False
    )
```

time: 1590 us -> 596 us (0.37)
  local copies, waits for them, and re-layouts: 671 us -> 206 us
  other arithmetic: 517 us -> 73.1 us
  matrix products: 189 us -> 44.1 us
  Pallas kernels: 0 us -> 123 us
  waiting for transfers between devices: 154 us -> 113 us
    add x1 -> x0, other arithmetic: 204 us -> none  [combine(): fourths + single_rate + doubled + tripled]
    concatenate x2 -> x7, other arithmetic: 213 us -> 21.9 us  [the longest x6 19.6 us: weights(): both = jnp.concatenate([upper, lower], axis=1)]
    another operation x12 -> x26, local copies, waits for them, and re-layouts: 228 us -> 41.3 us  [the longest x22 40.9 us: windows(): stretch[part, piece * step:(piece + blocks) * step].reshape(blocks, step)]
    add x3 -> x0, local copies, waits for them, and re-layouts: 140 us -> none  [combine(): fourths + single_rate + doubled + tripled]
    dot_general x4 -> x8, matrix products: 147 us -> 14.8 us  [weights(): jnp.einsum('ctmi,ml->ctil', half[..., :width], chosen, preferred_element_...]
    pallas_call x0 -> x2, Pallas kernels: none -> 123 us  [powers(): pl.pallas_call(functools.partial(power_kernel, count, int(base is not Non...]
    slice x12 -> x4, local copies, waits for them, and re-layouts: 144 us -> 48.9 us  [windows(): stretch[part, piece * step:(piece + blocks) * step].reshape(blocks, step)]
    transpose x4 -> x0, local copies, waits for them, and re-layouts: 79.8 us -> none  [the longest x2 78.6 us: correlate(): return jnp.transpose(powers, (1, 0, 2)).reshape(templates, length)]
  transfers between devices with their start and end apart: 9 -> 5, of which waited for: 5 -> 4; matrix products, arithmetic and copies ran while one was open for 16% -> 22% of each run, Pallas kernels for 0% -> 6%
where the time goes in v1:
time: 596 us; the launch traced here: 587 us
  local copies, waits for them, and re-layouts  206 us (35%)
  Pallas kernels  123 us (21%)
  waiting for transfers between devices  113 us (19%)
  other arithmetic  73.1 us (12%)
  matrix products  44.1 us (7%)
  starting transfers between devices  26.6 us (4%)
    pallas_call x2, Pallas kernels, powers(): pl.pallas_call(functools.partial(power_kernel, count, int(base is not Non...  123 us
    all_to_all x2, waiting for transfers between devices, fetched(): lax.all_to_all(jnp.stack(slabs), 'freq', split_axis=0, concat_axis=0, til...  63.2 us
    slice x4, local copies, waits for them, and re-layouts, windows(): stretch[part, piece * step:(piece + blocks) * step].reshape(blocks, step)  48.9 us
    another operation x22, local copies, waits for them, and re-layouts, windows(): stretch[part, piece * step:(piece + blocks) * step].reshape(blocks, step)  40.9 us
    gather x6, local copies, waits for them, and re-layouts, on_device(): chosen = jnp.take(matrices, sub_rows[harmonic - 1], axis=1)  31 us
    dot_general x12, matrix products, single(): return jnp.einsum(pattern, one_side, other_side, precision=highest)  26.5 us
    all_to_all x1, waiting for transfers between devices, forward_spectrum(): lax.all_to_all(arrange(columns[1]), 'freq', split_axis=0, concat_axis=0,...  25.6 us
    all_to_all x1, waiting for transfers between devices, forward_spectrum(): lax.all_to_all(arrange(columns[0]), 'freq', split_axis=0, concat_axis=0,...  24.3 us
  transfers between devices with their start and end apart: 5, of which 4 were waited for; matrix products, arithmetic and copies ran while one was open for 22% of the time, Pallas kernels for 6%

profile of v1, /device:TPU:1, one launch (start us, length us, event | category | flops | bytes accessed | tf_op | source)
XLA Modules:
  0.0 587.0 jit_solution(11822387700492358922)
XLA Ops:
  1.9 3.5 copy.112
  5.4 6.5 %all-to-all-start = ((f32[8,1,65536]{2,1,0:T(1,128)}), f32[8,1,65536]{2,1,0:T(1,128)}, u32[]{:S(2)}, u32[]{:S(2)}) async-start(f32[8,1,65536]{2,1,0:T(1,128)} %copy.112), calls=%async_computation | async-start | bytes 4194304 | tf_op jit(solution)/shard_map/all_to_all | solution.py:50
  12.1 3.1 tile.4
  15.2 6.7 %tile.10 = f32[2,16,32896]{2,1,0:T(8,128)} reshape(f32[2,16,128,257]{3,2,1,0:T(8,128)} %tile.4) | data formatting | bytes 8421376 | tf_op jit(solution)/shard_map/tile | solution.py:111
  24.1 3.3 copy.153
  27.4 4.9 gather_fusion.2
  32.3 5.3 copy.138
  37.6 6.6 %fusion.263 = (f32[2,16,128,256]{2,3,1,0:T(8,128)}, f32[2,16,128,256]{2,3,1,0:T(8,128)}) fusion(f32[16,2,128,256]{2,3,0,1:T(8,128)} %copy.138, pred[16]{0:T(512)(128)(4,1)S(1)} %get-tuple-element.30), kind=kLoop, calls=%fused_computation.421 | loop fusion | flops 2097152 | bytes 12582928 | tf_op jit(solution)/shard_map/reduce_precision | solution.py:116
  44.5 5.0 gather_fusion.1
  49.5 4.9 gather_fusion
  54.5 5.3 copy.136
  59.8 5.5 copy.137
  65.3 2.8 fusion.68
  69.7 3.0 fusion.65
  74.3 2.7 fusion.265
  83.9 6.6 %reduce = f32[8,65536]{1,0:T(8,128)S(1)} reduce(f32[8,1,65536]{2,1,0:T(1,128)} %all-to-all-done, f32[]{:T(128)} %constant.159), dimensions={1}, to_apply=%all_to_all.25.reduce_sub_computation | reduce | bytes 4194308 | tf_op jit(solution)/shard_map/all_to_all | solution.py:50
  93.3 2.6 fusion.50
  95.9 2.4 fusion.52
  98.3 2.5 subtract_bitcast_fusion
  100.9 2.6 add_bitcast_fusion
  106.3 10.0 %fusion.39 = (f32[8,256,256]{2,1,0:T(8,128)S(1)}, f32[8,256,256]{2,1,0:T(8,128)}) fusion(s32[8,256]{1,0:T(8,128)S(1)} %multiply_add_fusion.2, s32[256]{0:T(256)S(1)} %iota_add_fusion, f32[256,8,256]{0,2,1:T(8,128)S(1)} %bitcast.289, f32[256,8,256]{0,2,1:T(8,128)S(1)} %bitcast.290), kind=kLoop, calls=%fused_computation.129 | loop fusion | flops 10485760 | bytes 8397824 | tf_op jit(solution)/shard_map/transpose | solution.py:72
  116.3 4.2 all_to_all.32
  120.5 5.4 all-to-all-start.1
  129.2 2.4 convolution_convert_fusion.2
  143.3 6.6 %all_to_all.33 = f32[8,1,65536]{2,1,0:T(1,128)} reshape(f32[8,256,256]{2,1,0:T(8,128)} %get-tuple-element.45) | data formatting | bytes 4194304 | tf_op jit(solution)/shard_map/all_to_all | solution.py:78
  149.9 24.3 %all-to-all-done.1 = f32[8,1,65536]{2,1,0:T(1,128)} async-done(((f32[8,1,65536]{2,1,0:T(1,128)}), f32[8,1,65536]{2,1,0:T(1,128)}, u32[]{:S(2)}, u32[]{:S(2)}) %all-to-all-start.1) | async-done | bytes 2097184 | tf_op jit(solution)/shard_map/all_to_all | solution.py:77
  174.2 5.1 all-to-all-start.2
  183.6 3.9 maximum_maximum_fusion
  187.5 2.3 fusion.21.refs_8_
  190.6 2.5 fusion.18.refs_7_
  193.0 6.6 %reduce.1 = f32[8,65536]{1,0:T(8,128)S(1)} reduce(f32[8,1,65536]{2,1,0:T(1,128)} %all-to-all-done.1, f32[]{:T(128)} %constant.159), dimensions={1}, to_apply=%all_to_all.27.reduce_sub_computation | reduce | bytes 4194308 | tf_op jit(solution)/shard_map/all_to_all | solution.py:77
  199.6 2.3 fusion.180
  202.0 25.6 %all-to-all-done.2 = f32[8,1,65536]{2,1,0:T(1,128)} async-done(((f32[8,1,65536]{2,1,0:T(1,128)}), f32[8,1,65536]{2,1,0:T(1,128)}, u32[]{:S(2)}, u32[]{:S(2)}) %all-to-all-start.2) | async-done | bytes 2097184 | tf_op jit(solution)/shard_map/all_to_all | solution.py:78
  227.6 7.9 %reduce.2 = f32[8,65536]{1,0:T(8,128)} reduce(f32[8,1,65536]{2,1,0:T(1,128)} %all-to-all-done.2, f32[]{:T(128)} %constant.159), dimensions={1}, to_apply=%all_to_all.29.reduce_sub_computation | reduce | bytes 4194308 | tf_op jit(solution)/shard_map/all_to_all | solution.py:78
  235.5 3.2 fusion.178
  257.7 5.2 all-to-all-start.4
  263.2 3.5 maximum_maximum_fusion.3.refs_6_
  266.7 5.6 fusion.25
  275.1 39.0 %all-to-all-done.4 = f32[8,2,136,256]{3,2,1,0:T(8,128)} async-done(((f32[8,2,136,256]{3,2,1,0:T(8,128)}), f32[8,2,136,256]{3,2,1,0:T(8,128)}, u32[]{:S(2)}, u32[]{:S(2)}) %all-to-all-start.4) | async-done | bytes 2228256 | tf_op jit(solution)/shard_map/all_to_all | solution.py:249
  314.1 4.4 all-to-all-start.3
  322.3 8.8 %fusion.266 = (f32[1,262144]{1,0:T(1,128)S(1)}, f32[1,262144]{1,0:T(1,128)S(1)}, f32[1,262144]{1,0:T(1,128)S(1)}, f32[1,262144]{1,0:T(1,128)S(1)}) fusion(f32[2,266240]{1,0:T(2,128)S(1)} %bitcast.280), kind=kLoop, calls=%fused_computation.424 | loop fusion | bytes 8388608 | tf_op jit(solution)/shard_map/slice | solution.py:155
  331.1 2.2 pad_maximum_fusion.refs_0_
  333.3 34.4 %shard_map.82.refs_9_ = f32[16,262144]{1,0:T(8,128)} custom-call(f32[2048,512]{1,0:T(8,128)} %pad_maximum_fusion.refs_0_, bf16[16,512,256]{2,1,0:T(8,128)(2,1)} %get-tuple-element.104.refs_1_, bf16[16,512,256]{2,1,0:T(8,128)(2,1)} %get-tuple-element.105.refs_2_), custom_call_target="tpu_custom_call" | custom-call | flops 25769803776 | bytes 25165824 | tf_op jit(solution)/shard_map/pallas_call | solution.py:221
  367.8 24.3 %all-to-all-done.3 = f32[8,2,200,256]{3,2,1,0:T(8,128)S(1)} async-done(((f32[8,2,200,256]{3,2,1,0:T(8,128)}), f32[8,2,200,256]{3,2,1,0:T(8,128)S(1)}, u32[]{:S(2)}, u32[]{:S(2)}) %all-to-all-start.3) | async-done | bytes 3276832 | tf_op jit(solution)/shard_map/all_to_all | solution.py:249
  395.3 12.2 %slice_reduce_fusion.6 = (f32[131072]{0:T(1024)}, f32[131072]{0:T(1024)}, f32[131072]{0:T(1024)}, f32[131072]{0:T(1024)}, f32[131072]{0:T(1024)S(1)}, /*index=5*/f32[131072]{0:T(1024)S(1)}) fusion(f32[2,135168]{1,0:T(2,128)S(1)} %bitcast.283), kind=kLoop, calls=%fused_computation.203 | loop fusion | bytes 6291456 | tf_op jit(solution)/shard_map/slice | solution.py:155
  407.6 2.3 reshape_squeeze.93
  409.8 2.2 reshape_squeeze.92
  412.0 2.2 reshape_squeeze.91
  414.3 2.3 reshape_squeeze.90
  418.9 9.7 %slice_reduce_fusion.12 = (f32[65536]{0:T(1024)}, f32[65536]{0:T(1024)}, f32[65536]{0:T(1024)}, f32[65536]{0:T(1024)}, f32[65536]{0:T(1024)}, /*index=5*/f32[655...) fusion(f32[2,69632]{1,0:T(2,128)S(1)} %bitcast.281), kind=kLoop, calls=%fused_computation.251 | loop fusion | bytes 5242880 | tf_op jit(solution)/shard_map/slice | solution.py:155
  429.8 2.3 reshape_squeeze.86
  432.1 2.2 reshape_squeeze.85
  434.3 2.2 reshape_squeeze.84
  436.5 2.2 reshape_squeeze.83
  438.7 2.2 reshape_squeeze.82
  440.9 2.2 reshape_squeeze.81
  446.9 18.2 %slice_reduce_fusion = (f32[196608]{0:T(1024)}, f32[196608]{0:T(1024)}, f32[196608]{0:T(1024)}, f32[196608]{0:T(1024)}, f32[196608]{0:T(1024)}, /*index=5*/f32[196608]{0:T(1024)S(1)}) fusion(f32[2,200704]{1,0:T(2,128)S(1)} %bitcast.273), kind=kLoop, calls=%fused_computation.192 | loop fusion | bytes 9437184 | tf_op jit(solution)/shard_map/slice | solution.py:155
  465.1 2.5 reshape_squeeze.99
  467.6 2.5 reshape_squeeze.98
  472.6 2.5 reshape_squeeze.95
  476.4 6.0 %concatenate.141.refs_1_ = f32[2048,384]{1,0:T(8,128)} concatenate(f32[2048,64]{1,0:T(8,128)} %reshape_squeeze.88, f32[2048,64]{1,0:T(8,128)} %reshape_squeeze.89, f32[2048,64]{1,0:T(8,128)} %reshape_squeeze.90, f32[2048,64]{1,0:T(8,128)} %reshape_squeeze.91, f32[2048,64]{1,0:T(8,128)} %reshape_squeeze.92, f32[2048,64]{1,0:T(8,128)S(1)} %copy-done.23), dimensions={1} | concatenate | bytes 6291456 | tf_op jit(solution)/shard_map/concatenate | solution.py:160
  482.4 7.2 %concatenate.142.refs_2_ = f32[2048,512]{1,0:T(8,128)} concatenate(f32[2048,96]{1,0:T(8,128)} %reshape_squeeze.94, f32[2048,96]{1,0:T(8,128)} %reshape_squeeze.95, f32[2048,32]{1,0:T(8,128)} %bitcast.295, f32[2048,96]{1,0:T(8,128)} %reshape_squeeze.97, f32[2048,96]{1,0:T(8,128)} %reshape_squeeze.98, f32[2048,32]{1,0:T(8,128)} %bitcast.294, f32[2048,64]{1,0:T(8,128)S(1)} %broadcast.273), dimensions={1} | concatenate | bytes 8388608 | tf_op jit(solution)/shard_map/concatenate | solution.py:160
  489.6 8.5 %concatenate.140.refs_0_ = f32[2048,384]{1,0:T(8,128)} concatenate(f32[2048,32]{1,0:T(8,128)} %reshape_squeeze.78, f32[2048,32]{1,0:T(8,128)} %reshape_squeeze.79, f32[2048,32]{1,0:T(8,128)} %reshape_squeeze.80, f32[2048,32]{1,0:T(8,128)} %reshape_squeeze.81, f32[2048,32]{1,0:T(8,128)} %reshape_squeeze.82, f32[2048,32]{1,0:T(8,128)} %reshape_squeeze.83, ...), dimensions={1} | concatenate | bytes 6291456 | tf_op jit(solution)/shard_map/concatenate | solution.py:160
  498.1 88.8 %shard_map.83 = f32[16,262144]{1,0:T(8,128)} custom-call(f32[2048,384]{1,0:T(8,128)} %concatenate.140.refs_0_, f32[2048,384]{1,0:T(8,128)} %concatenate.141.refs_1_, f32[2048,512]{1,0:T(8,128)} %concatenate.142.refs_2_, bf16[16,384,256]{2,1,0:T(8,128)(2,1)} %get-tuple-element.106.refs_3_, ...), custom_call_target="tpu_custom_call", output_to_operand_aliasing={{}: (9, {})} | custom-call | flops 64424509440 | bytes 37748736 | tf_op jit(solution)/shard_map/pallas_call | solution.py:221
  (183 shorter events, 80.1 us)
Async XLA Ops:
  5.3 6.6 %copy-start.41 = (s32[3,16]{1,0:T(4,128)S(1)}, s32[3,16]{1,0:T(4,128)}, u32[]{:S(2)}) copy-start(s32[3,16]{1,0:T(4,128)} %param.13) | copy-start | bytes 580
  5.3 6.6 %copy-start.42 = (s32[16]{0:T(128)S(1)}, s32[16]{0:T(128)}, u32[]{:S(2)}) copy-start(s32[16]{0:T(128)} %param.12) | copy-start | bytes 196
  5.4 6.7 %copy-start.40 = (f32[2,16,129]{2,1,0:T(8,128)S(1)}, f32[2,16,129]{2,1,0:T(8,128)}, u32[]{:S(2)}) copy-start(f32[2,16,129]{2,1,0:T(8,128)} %param.11) | copy-start | bytes 49540
  5.4 78.6 %all-to-all-start = ((f32[8,1,65536]{2,1,0:T(1,128)}), f32[8,1,65536]{2,1,0:T(1,128)}, u32[]{:S(2)}, u32[]{:S(2)}) async-start(f32[8,1,65536]{2,1,0:T(1,128)} %copy.112), calls=%async_computation | async-start | bytes 4194304 | tf_op jit(solution)/shard_map/all_to_all | solution.py:50
  21.9 2.2 slice-start
  59.8 5.5 copy-start.39
  65.3 4.4 copy-start.1
  68.2 1.5 copy-start.10
  69.7 4.6 copy-start.6
  72.7 1.6 copy-start.9
  74.3 2.8 copy-start.37
  74.3 5.1 copy-start.5
  77.0 2.3 copy-start.2
  79.4 1.1 copy-start.38
  120.5 5.4 copy-start.14
  120.5 5.5 copy-start.12
  120.5 53.7 %all-to-all-start.1 = ((f32[8,1,65536]{2,1,0:T(1,128)}), f32[8,1,65536]{2,1,0:T(1,128)}, u32[]{:S(2)}, u32[]{:S(2)}) async-start(f32[8,1,65536]{2,1,0:T(1,128)} %all_to_all.32), calls=%async_computation.1 | async-start | bytes 4194304 | tf_op jit(solution)/shard_map/all_to_all | solution.py:77
  125.9 1.6 copy-start.17
  126.0 3.3 copy-start.3
  129.2 4.0 copy-start
  131.7 1.5 copy-start.19
  131.7 1.5 copy-start.36
  134.0 2.0 copy-start.7
  136.0 1.8 copy-start.15
  137.9 2.0 copy-start.13
  139.8 2.1 copy-start.11
  149.9 29.4 %copy-start.18 = (bf16[2,16,160,128]{3,2,1,0:T(8,128)(2,1)S(1)}, bf16[2,16,160,128]{3,2,1,0:T(8,128)(2,1)}, u32[]{:S(2)}) copy-start(bf16[2,16,160,128]{3,2,1,0:T(8,128)(2,1)} %convolution_convert_fusion.3) | copy-start | bytes 3932164
  174.2 53.4 %all-to-all-start.2 = ((f32[8,1,65536]{2,1,0:T(1,128)}), f32[8,1,65536]{2,1,0:T(1,128)}, u32[]{:S(2)}, u32[]{:S(2)}) async-start(f32[8,1,65536]{2,1,0:T(1,128)} %all_to_all.33), calls=%async_computation.2 | async-start | bytes 4194304 | tf_op jit(solution)/shard_map/all_to_all | solution.py:78
  179.3 2.6 copy-start.8
  182.0 1.2 copy-start.21
  182.1 1.5 copy-start.22
  183.6 3.9 copy-start.28
  187.5 2.3 copy-start.25
  187.5 2.3 copy-start.26
  187.5 3.1 copy-start.27
  235.5 3.2 copy-start.4
  235.5 3.2 copy-start.16
  251.2 0.7 copy-start.43
  257.7 5.2 copy-start.20
  257.7 56.4 %all-to-all-start.4 = ((f32[8,2,136,256]{3,2,1,0:T(8,128)}), f32[8,2,136,256]{3,2,1,0:T(8,128)}, u32[]{:S(2)}, u32[]{:S(2)}) async-start(f32[8,2,136,256]{3,2,1,0:T(8,128)} %fusion.108), calls=%async_computation.4 | async-start | bytes 4456448 | tf_op jit(solution)/shard_map/all_to_all | solution.py:249
  263.2 3.5 copy-start.31
  263.2 3.5 copy-start.32
  263.2 3.5 copy-start.33
  263.2 3.6 copy-start.34
  263.2 3.6 copy-start.35
  273.5 1.7 copy-start.24
  314.1 77.9 %all-to-all-start.3 = ((f32[8,2,200,256]{3,2,1,0:T(8,128)}), f32[8,2,200,256]{3,2,1,0:T(8,128)S(1)}, u32[]{:S(2)}, u32[]{:S(2)}) async-start(f32[8,2,200,256]{3,2,1,0:T(8,128)} %copy-done.24), calls=%async_computation.3 | async-start | bytes 6553600 | tf_op jit(solution)/shard_map/all_to_all | solution.py:249
  465.1 5.0 copy-start.30
  467.6 3.7 copy-start.29
  472.6 3.8 copy-start.23
